TPU v7x, 256 devices: a whole 4x4x8 slice. The times are simulated.
256 devices in a mesh: pb: 32 (over y, x, core), ka: 8 (over z).
Axes of the slice: x: 4, y: 4, z: 8, core: 2. Of those that a mesh axis runs over, the one named last changes fastest.
Arguments:
- queries: bfloat16 [16384, 1024], P('pb'), may hold values from -8 to 8
- keys: bfloat16 [8, 2048, 128], P('ka', 'pb'), may hold values from -4 to 4
- values: bfloat16 [8, 2048, 128], P('ka', 'pb'), may hold values from -4 to 4
- span_of: int32 [64], replicated, may hold values from 0 to 63, as said below
Outputs:
- attended: bfloat16 [16384, 1024], P('pb', 'ka')
- log_norm: float32 [8, 16384], P('ka', 'pb')
Inputs may be any that keep to these rules, and one draw needn't show every extreme that they name: `span_of`: for each index p of pb, slots 2 p and 2 p + 1 hold a span c and its mirror 64 - 1 - c, in either order; every span is held once.
All inputs are finite; a program needn't handle non-finite values.
Results may differ from a plain program's by a relative error of at most 0.018.
Values may be sent and summed in bfloat16 or wider, within the bound.
No kernel may reach another device: no remote copies, remote signals or barrier semaphores. Data moves between devices by JAX's collectives and lax.ppermute only.
A program may use at most 128 MiB of HBM per device.

v0:
```python
import math
import jax
import jax.numpy as jnp
from jax import lax
from jax.sharding import PartitionSpec as P

NEG = -1e30


def lookup(table, index):
    match = index[:, None] == jnp.arange(table.shape[0], dtype=jnp.int32)[None, :]
    return jnp.sum(jnp.where(match, table[None, :], 0), axis=1)


def update(state, block_keys, block_values, block_pos, query_flat, pos_flat, scale):
    best, total, accum = state
    scores = (
        lax.dot_general(
            query_flat, block_keys, (((1,), (1,)), ((), ())), preferred_element_type=jnp.float32
        )
        * scale
    )
    seen = block_pos[None, :] <= pos_flat[:, None]
    newbest = jnp.maximum(best, jnp.max(jnp.where(seen, scores, NEG), axis=1))
    factor = jnp.exp(best - newbest)
    weights = jnp.where(seen, jnp.exp(scores - newbest[:, None]), 0.0)
    total = total * factor + jnp.sum(weights, axis=1)
    accum = accum * factor[:, None] + jnp.dot(
        weights.astype(jnp.bfloat16), block_values, preferred_element_type=jnp.float32
    )
    return (newbest, total, accum)


def local(queries, keys, values, span_of):
    group = lax.axis_index("ka")
    groups = lax.axis_size("ka")
    place = lax.axis_index("pb")
    rows, width = queries.shape
    head_dim = keys.shape[2]
    heads = width // head_dim
    per_span = rows // 2
    key_rows = per_span // groups
    scale = 1.0 / math.sqrt(head_dim)
    local_spans = lookup(span_of, 2 * place + jnp.arange(2, dtype=jnp.int32))
    query_pos = (
        local_spans[:, None] * per_span + jnp.arange(per_span, dtype=jnp.int32)[None, :]
    ).reshape(rows)
    flat_queries = queries.reshape(rows * heads, head_dim)
    flat_pos = jnp.repeat(query_pos, heads)
    count = rows * heads
    state = (
        jnp.full((count,), NEG, jnp.float32),
        jnp.zeros((count,), jnp.float32),
        jnp.zeros((count, head_dim), jnp.float32),
    )
    start = jnp.int32(0)
    piece_keys = lax.all_gather(keys, "pb", axis=1, tiled=True)[0]
    piece_values = lax.all_gather(values, "pb", axis=1, tiled=True)[0]
    absorb_count = piece_keys.shape[0]
    step = min(absorb_count, 512)
    for first in range(0, absorb_count, step):
        size = min(step, absorb_count - first)
        index = start + first + jnp.arange(size, dtype=jnp.int32)
        block_pos = (
            lookup(span_of, index // key_rows) * per_span + index % key_rows * groups + group
        )
        state = update(
            state,
            piece_keys[first : first + size],
            piece_values[first : first + size],
            block_pos,
            flat_queries,
            flat_pos,
            scale,
        )
    best, total, accum = state
    partial_value = (
        (accum / jnp.maximum(total, 1.0)[:, None]).astype(jnp.bfloat16).reshape(rows, width)
    )
    best = best.reshape(rows, heads)
    total = total.reshape(rows, heads)
    local_heads = heads // groups
    received = lax.all_to_all(
        partial_value.reshape(1, rows, width), "ka", split_axis=2, concat_axis=0, tiled=True
    )
    got_best, got_total = (
        lax.all_to_all(best.reshape(1, rows, heads), "ka", split_axis=2, concat_axis=0, tiled=True),
        lax.all_to_all(
            total.reshape(1, rows, heads), "ka", split_axis=2, concat_axis=0, tiled=True
        ),
    )
    top = jnp.max(got_best, axis=0)
    share = got_total * jnp.exp(got_best - top)
    norm = jnp.sum(share, axis=0)
    pieces = received.reshape(groups, rows, local_heads, head_dim).astype(jnp.float32)
    merged = jnp.sum(share[..., None] * pieces, axis=0) / norm[..., None]
    attended = merged.reshape(rows, local_heads * head_dim).astype(jnp.bfloat16)
    log_norm = (top + jnp.log(norm)).T
    return (attended, log_norm)


def solution(mesh):
    placed = (P("pb", None), P("ka", "pb", None), P("ka", "pb", None), P())
    return jax.shard_map(
        local, mesh=mesh, in_specs=placed, out_specs=(P("pb", "ka"), P("ka", "pb")), check_vma=False
    )
```

profile of v0, /device:TPU:1, one launch (start us, length us, event | category | flops | bytes accessed | tf_op | source)
XLA Modules:
  0.0 185.1 jit_solution(387766933692637548)
XLA Ops:
  0.7 1.5 reshape.520
  2.2 26.4 %all_gather.6 = bf16[1,2048,128]{2,1,0:T(8,128)(2,1)S(1)} all-gather(bf16[1,64,128]{2,1,0:T(8,128)(2,1)} %param.5), channel_id=1, replica_groups=mesh['pb'=32,'ka'=8] {'pb'}, dimensions={1}, use_global_device_ids=true | all-gather | bytes 540672 | tf_op jit(solution)/shard_map/all_gather | solution.py:57
  28.6 4.5 %fusion.38 = f32[4096,512]{0,1:T(8,128)} fusion(bf16[4096,128]{1,0:T(8,128)(2,1)S(1)} %reshape.520, bf16[1,2048,128]{2,1,0:T(8,128)(2,1)S(1)} %all_gather.6), kind=kOutput, calls=%fused_computation.53 | convolution fusion | flops 536870912 | bytes 9568256 | tf_op jit(solution)/shard_map/dot_general | solution.py:18
  33.1 4.5 %fusion.39 = f32[4096,512]{0,1:T(8,128)} fusion(bf16[4096,128]{1,0:T(8,128)(2,1)S(1)} %reshape.520, bf16[1,2048,128]{2,1,0:T(8,128)(2,1)S(1)} %all_gather.6), kind=kOutput, calls=%fused_computation.55 | convolution fusion | flops 536870912 | bytes 9568256 | tf_op jit(solution)/shard_map/dot_general | solution.py:18
  37.6 0.2 fusion.75
  37.9 0.1 broadcast_in_dim.101
  38.0 0.2 le.21
  38.1 0.2 select_reduce_fusion
  38.3 4.5 %fusion = (f32[4096]{0:T(1024)S(1)}, f32[4096,512]{0,1:T(8,128)}) fusion(s32[4096]{0:T(1024)S(1)} %le.21, s32[512]{0:T(512)S(1)} %get-tuple-element.37, bf16[4096,128]{1,0:T(8,128)(2,1)S(1)} %reshape.520, bf16[1,2048,128]{2,1,0:T(8,128)(2,1)S(1)} %all_gather.6), kind=kOutput, calls=%fused_computation.8 | convolution fusion | flops 545255424 | bytes 9603072 | tf_op jit(solution)/shard_map/dot_general | solution.py:18
  42.9 0.2 max_broadcast_in_dim.46
  43.0 16.2 %fusion.5 = (f32[4096]{0:T(1024)S(1)}, f32[4096]{0:T(1024)S(1)}, f32[4096]{0:T(1024)S(1)}, f32[4096]{0:T(1024)S(1)}, f32[4096,512]{0,1:T(8,128)}) fusion(f32[4096,512]{0,1:T(8,128)} %get-tuple-element.32, f32[4096]{0:T(1024)S(1)} %broadcast_maximum_fusion, s32[4096]{0:T(1024)S(1)} %le.21, s32[512]{0:T(512)S(1)} %get-tuple-element.37, ...), kind=kOutput, calls=%fused_computation.13 | convolution fusion | flops 572506112 | bytes 34840576 | tf_op jit(solution)/shard_map/dot_general | solution.py:18
  59.3 0.2 reduce_max.53
  59.4 0.2 reduce_max.55
  59.6 0.2 reduce_max.57
  59.8 0.1 copy.20
  59.9 0.1 copy.23
  60.0 0.1 copy.17
  60.1 11.3 %fusion.7 = (f32[4096]{0:T(1024)S(1)}, f32[4096]{0:T(1024)S(1)}, f32[4096]{0:T(1024)S(1)}) fusion(f32[4096,512]{0,1:T(8,128)} %get-tuple-element.33, f32[4096]{0:T(1024)S(1)} %get-tuple-element.29, s32[4096]{0:T(1024)S(1)} %le.21, s32[512]{0:T(512)S(1)} %get-tuple-element.34, f32[4096]{0:T(1024)S(1)} %get-tuple-element.27, f32[4096,512]{0,1:T(8,128)} %fusion.38, ...), kind=kLoop, calls=%fused_computation.15 | loop fusion | flops 31444992 | bytes 25286656 | tf_op jit(solution)/shard_map/reduce_sum | solution.py:27
  71.4 0.2 reduce_sum.113
  71.6 0.1 copy.22
  71.6 0.2 reduce_sum.116
  71.8 0.1 copy.24
  71.9 0.2 reduce_sum.119
  72.1 0.1 copy.26
  72.2 0.2 reduce_sum.110
  72.4 0.1 copy.18
  72.5 0.1 copy.25
  72.6 0.6 copy.28
  73.2 8.2 %all-to-all-start.1 = ((f32[1,512,8]{1,0,2:T(1,128)}), f32[1,512,8]{1,0,2:T(1,128)S(1)}, u32[]{:S(2)}, u32[]{:S(2)}) async-start(f32[1,512,8]{1,0,2:T(1,128)} %copy.28), calls=%async_computation.1 | async-start | bytes 32768 | tf_op jit(solution)/shard_map/all_to_all | solution.py:87
  81.5 24.7 %all_gather.7 = bf16[1,2048,128]{2,1,0:T(8,128)(2,1)S(1)} all-gather(bf16[1,64,128]{2,1,0:T(8,128)(2,1)S(1)} %copy-done), channel_id=1, replica_groups=mesh['pb'=32,'ka'=8] {'pb'}, dimensions={1}, use_global_device_ids=true | all-gather | bytes 540672 | tf_op jit(solution)/shard_map/all_gather | solution.py:58
  106.2 5.6 %fusion.14 = f32[4096,128]{1,0:T(8,128)S(1)} fusion(f32[4096,512]{0,1:T(8,128)} %get-tuple-element.32, f32[4096]{0:T(1024)S(1)} %broadcast_maximum_fusion, s32[4096]{0:T(1024)S(1)} %le.21, s32[512]{0:T(512)S(1)} %get-tuple-element.37, f32[4096]{0:T(1024)S(1)} %get-tuple-element.26, f32[4096]{0:T(1024)S(1)} %get-tuple-element.30, ...), kind=kOutput, calls=%fused_computation.26 | convolution fusion | flops 548405248 | bytes 10684416 | tf_op jit(solution)/shard_map/dot_general | solution.py:28
  111.8 2.5 %fusion.13 = f32[4096,128]{1,0:T(8,128)S(1)} fusion(f32[4096,128]{1,0:T(8,128)S(1)} %fusion.14, f32[4096,512]{0,1:T(8,128)S(1)} %bitcast.78, f32[4096]{0:T(1024)S(1)} %get-tuple-element.29, s32[4096]{0:T(1024)S(1)} %le.21, s32[512]{0:T(512)S(1)} %get-tuple-element.34, f32[4096]{0:T(1024)S(1)} %get-tuple-element.25, bf16[1,2048,128]{2,1,0:T(8,128)(2,1)S(1)} %all_gather.7), kind=kOutput, calls=%fused_computation.24 | convolution fusion | flops 548405248 | bytes 12765184 | tf_op jit(solution)/shard_map/dot_general | solution.py:28
  114.3 0.9 slice-done.1
  115.3 3.9 %fusion.12 = f32[4096,128]{1,0:T(8,128)} fusion(f32[4096,128]{1,0:T(8,128)S(1)} %fusion.13, f32[4096,512]{0,1:T(8,128)S(1)} %bitcast.75, f32[4096]{0:T(1024)S(1)} %get-tuple-element.28, s32[4096]{0:T(1024)S(1)} %le.21, s32[512]{0:T(512)S(1)} %get-tuple-element.35, f32[4096]{0:T(1024)S(1)} %get-tuple-element.24, bf16[1,2048,128]{2,1,0:T(8,128)(2,1)S(1)} %all_gather.7), kind=kOutput, calls=%fused_computation.22 | convolution fusion | flops 548405248 | bytes 12765184 | tf_op jit(solution)/shard_map/dot_general | solution.py:28
  119.1 0.6 copy.27
  119.8 6.9 %all-to-all-start = ((f32[1,512,8]{1,0,2:T(1,128)}), f32[1,512,8]{1,0,2:T(1,128)S(1)}, u32[]{:S(2)}, u32[]{:S(2)}) async-start(f32[1,512,8]{1,0,2:T(1,128)} %copy.27), calls=%async_computation | async-start | bytes 32768 | tf_op jit(solution)/shard_map/all_to_all | solution.py:88
  126.7 6.5 %fusion.16 = bf16[4096,128]{1,0:T(8,128)(2,1)S(1)} fusion(f32[4096,128]{1,0:T(8,128)} %fusion.12, f32[4096,512]{0,1:T(8,128)} %fusion.38, f32[4096]{0:T(1024)S(1)} %get-tuple-element.27, s32[4096]{0:T(1024)S(1)} %le.21, s32[512]{0:T(512)S(1)} %get-tuple-element.36, f32[4096]{0:T(1024)S(1)} %get-tuple-element.23, bf16[1,2048,128]{2,1,0:T(8,128)(2,1)S(1)} %all_gather.7), kind=kOutput, calls=%fused_computation.28 | convolution fusion | flops 548929536 | bytes 11716608 | tf_op jit(solution)/shard_map/dot_general | solution.py:28
  133.2 0.5 reshape_reshape.2
  133.7 1.8 copy.29
  135.5 0.5 broadcast.448
  136.0 7.0 %reduce.6 = bf16[1024,512]{1,0:T(8,128)(2,1)S(1)} reduce(bf16[1024,1,512]{2,1,0:T(2,128)(2,1)S(1)} %bitcast.79, bf16[]{:T(256)} %broadcast.448), dimensions={1}, to_apply=%bitcast.64.reduce_sub_computation | reduce | bytes 2097154
  143.1 1.6 reshape.523
  144.7 6.6 %all-to-all-start.2 = ((bf16[8,2,32768]{2,1,0:T(2,128)(2,1)}), bf16[8,2,32768]{2,1,0:T(2,128)(2,1)S(1)}, u32[]{:S(2)}, u32[]{:S(2)}) async-start(bf16[8,2,32768]{2,1,0:T(2,128)(2,1)} %reshape.523), calls=%async_computation.2 | async-start | bytes 2097152 | tf_op jit(solution)/shard_map/all_to_all | solution.py:83
  151.4 0.6 log_add_fusion
  152.0 28.6 %all-to-all-done.2 = bf16[8,2,32768]{2,1,0:T(2,128)(2,1)S(1)} async-done(((bf16[8,2,32768]{2,1,0:T(2,128)(2,1)}), bf16[8,2,32768]{2,1,0:T(2,128)(2,1)S(1)}, u32[]{:S(2)}, u32[]{:S(2)}) %all-to-all-start.2) | async-done | bytes 1048608 | tf_op jit(solution)/shard_map/all_to_all | solution.py:83
  180.6 1.0 reshape.524
  181.6 2.7 %fusion.37 = f32[512,128]{0,1:T(8,128)S(1)} fusion(bf16[1,512,8,128]{1,0,3,2:T(2,128)(2,1)S(1)} %bitcast.76, f32[8,512]{1,0:T(8,128)S(1)} %fusion.43), kind=kLoop, calls=%fused_computation.46 | loop fusion | flops 1507328 | bytes 1327104 | tf_op jit(solution)/shard_map/reduce_sum | solution.py:96
  184.3 0.8 copy.30
  (34 shorter events, 0.4 us)
Async XLA Ops:
  33.1 4.5 %copy-start.1 = (s32[64]{0:T(128)S(1)}, s32[64]{0:T(128)}, u32[]{:S(2)}) copy-start(s32[64]{0:T(128)} %param.7) | copy-start | bytes 772
  60.1 21.4 %copy-start = (bf16[1,64,128]{2,1,0:T(8,128)(2,1)S(1)}, bf16[1,64,128]{2,1,0:T(8,128)(2,1)}, u32[]{:S(2)}) copy-start(bf16[1,64,128]{2,1,0:T(8,128)(2,1)} %param.6) | copy-start | bytes 49156
  73.2 46.5 %all-to-all-start.1 = ((f32[1,512,8]{1,0,2:T(1,128)}), f32[1,512,8]{1,0,2:T(1,128)S(1)}, u32[]{:S(2)}, u32[]{:S(2)}) async-start(f32[1,512,8]{1,0,2:T(1,128)} %copy.28), calls=%async_computation.1 | async-start | bytes 32768 | tf_op jit(solution)/shard_map/all_to_all | solution.py:87
  81.4 30.4 %slice-start.2 = ((s8[8388608]{0:T(1024)(128)(4,1)}), s8[4194304]{0:T(1024)(128)(4,1)S(1)}, s32[]{:S(2)}) async-start(s8[8388608]{0:T(1024)(128)(4,1)} %bitcast.77), calls=%async_computation.5 | async-start | bytes 8388608
  106.2 5.7 %slice-start.3 = ((s8[8388608]{0:T(1024)(128)(4,1)}), s8[4194304]{0:T(1024)(128)(4,1)S(1)}, s32[]{:S(2)}) async-start(s8[8388608]{0:T(1024)(128)(4,1)} %bitcast.77), calls=%async_computation.6 | async-start | bytes 8388608
  111.8 2.5 %slice-start = ((s8[8388608]{0:T(1024)(128)(4,1)}), s8[4194304]{0:T(1024)(128)(4,1)S(1)}, s32[]{:S(2)}) async-start(s8[8388608]{0:T(1024)(128)(4,1)} %bitcast.74), calls=%async_computation.3 | async-start | bytes 8388608
  111.8 3.4 %slice-start.1 = ((s8[8388608]{0:T(1024)(128)(4,1)}), s8[4194304]{0:T(1024)(128)(4,1)S(1)}, s32[]{:S(2)}) async-start(s8[8388608]{0:T(1024)(128)(4,1)} %bitcast.74), calls=%async_computation.4 | async-start | bytes 8388608
  119.8 24.9 %all-to-all-start = ((f32[1,512,8]{1,0,2:T(1,128)}), f32[1,512,8]{1,0,2:T(1,128)S(1)}, u32[]{:S(2)}, u32[]{:S(2)}) async-start(f32[1,512,8]{1,0,2:T(1,128)} %copy.27), calls=%async_computation | async-start | bytes 32768 | tf_op jit(solution)/shard_map/all_to_all | solution.py:88
  144.7 35.9 %all-to-all-start.2 = ((bf16[8,2,32768]{2,1,0:T(2,128)(2,1)}), bf16[8,2,32768]{2,1,0:T(2,128)(2,1)S(1)}, u32[]{:S(2)}, u32[]{:S(2)}) async-start(bf16[8,2,32768]{2,1,0:T(2,128)(2,1)} %reshape.523), calls=%async_computation.2 | async-start | bytes 2097152 | tf_op jit(solution)/shard_map/all_to_all | solution.py:83
where the time goes:
time: 185 us
  blocking collectives  51.1 us (28%)
  matrix products  48.1 us (26%)
  waiting for transfers between devices  28.6 us (15%)
  other arithmetic  22.3 us (12%)
  starting transfers between devices  21.8 us (12%)
  local copies, waits for them, and re-layouts  12.3 us (7%)
    dot_general x4, matrix products, update(): lax.dot_general(query_flat, block_keys, (((1,), (1,)), ((), ())), preferr...  29.7 us
    all_to_all x1, waiting for transfers between devices, local(): lax.all_to_all(partial_value.reshape(1, rows, width), 'ka', split_axis=2,...  28.6 us
    all_gather x1, blocking collectives, local(): piece_keys = lax.all_gather(keys, 'pb', axis=1, tiled=True)[0]  26.4 us
    all_gather x1, blocking collectives, local(): piece_values = lax.all_gather(values, 'pb', axis=1, tiled=True)[0]  24.7 us
    dot_general x4, matrix products, update(): jnp.dot(weights.astype(jnp.bfloat16), block_values, preferred_element_typ...  18.4 us
    reduce_sum x1, other arithmetic, update(): total = total * factor + jnp.sum(weights, axis=1)  11.3 us
    all_to_all x1, starting transfers between devices, local(): lax.all_to_all(best.reshape(1, rows, heads), 'ka', split_axis=2, concat_a...  8.19 us
    unnamed x4, other arithmetic  7.12 us
  transfers between devices with their start and end apart: 3, of which 1 were waited for; matrix products, arithmetic and copies ran while one was open for 17% of the time, Pallas kernels for 0%

commit v1 on v0

--- a/solution.py
+++ b/solution.py
@@ -80,8 +80,16 @@
     best = best.reshape(rows, heads)
     total = total.reshape(rows, heads)
     local_heads = heads // groups
-    received = lax.all_to_all(
-        partial_value.reshape(1, rows, width), "ka", split_axis=2, concat_axis=0, tiled=True
+    received = jnp.concatenate(
+        lax.all_to_all(
+            jnp.stack(
+                jnp.split(partial_value.reshape(1, rows, width), lax.axis_size("ka"), axis=2)
+            ),
+            "ka",
+            0,
+            0,
+        ),
+        axis=0,
     )
     got_best, got_total = (
         lax.all_to_all(best.reshape(1, rows, heads), "ka", split_axis=2, concat_axis=0, tiled=True),

time: 185 us -> 172 us (0.930)
  other arithmetic: 22.3 us -> 14 us
  matrix products: 48.1 us -> 42.8 us
  waiting for transfers between devices: 28.6 us -> 32.2 us
  starting transfers between devices: 21.8 us -> 18.7 us
    unnamed x4, other arithmetic: 7.12 us -> 0.08 us
    all_to_all x1, waiting for transfers between devices: 0.01 us -> 5.93 us  [local(): lax.all_to_all(total.reshape(1, rows, heads), 'ka', split_axis=2, concat_...]
    dot_general x4, matrix products: 18.4 us -> 13.5 us  [update(): jnp.dot(weights.astype(jnp.bfloat16), block_values, preferred_element_typ...]
    all_to_all x1, starting transfers between devices: 6.65 us -> 3.56 us  [local(): lax.all_to_all(jnp.stack(jnp.split(partial_value.reshape(1, rows, width),...]
    all_to_all x1, waiting for transfers between devices: 28.6 us -> 26.3 us  [local(): lax.all_to_all(jnp.stack(jnp.split(partial_value.reshape(1, rows, width),...]
    reduce_sum x1, other arithmetic: 2.66 us -> 0.7 us  [local(): merged = jnp.sum(share[..., None] * pieces, axis=0) / norm[..., None]]
    unnamed x17 -> x24, local copies, waits for them, and re-layouts: 4.88 us -> 5.69 us
  transfers between devices with their start and end apart: 3 -> 3, of which waited for: 1 -> 2; matrix products, arithmetic and copies ran while one was open for 17% -> 12% of each run, Pallas kernels for 0% -> 0%
where the time goes in v1:
time: 172 us
  blocking collectives  51.1 us (30%)
  matrix products  42.8 us (25%)
  waiting for transfers between devices  32.2 us (19%)
  starting transfers between devices  18.7 us (11%)
  other arithmetic  14 us (8%)
  local copies, waits for them, and re-layouts  12 us (7%)
    dot_general x4, matrix products, update(): lax.dot_general(query_flat, block_keys, (((1,), (1,)), ((), ())), preferr...  29.3 us
    all_gather x1, blocking collectives, local(): piece_keys = lax.all_gather(keys, 'pb', axis=1, tiled=True)[0]  26.4 us
    all_to_all x1, waiting for transfers between devices, local(): lax.all_to_all(jnp.stack(jnp.split(partial_value.reshape(1, rows, width),...  26.3 us
    all_gather x1, blocking collectives, local(): piece_values = lax.all_gather(values, 'pb', axis=1, tiled=True)[0]  24.7 us
    dot_general x4, matrix products, update(): jnp.dot(weights.astype(jnp.bfloat16), block_values, preferred_element_typ...  13.5 us
    reduce_sum x1, other arithmetic, update(): total = total * factor + jnp.sum(weights, axis=1)  11.3 us
    all_to_all x1, starting transfers between devices, local(): lax.all_to_all(best.reshape(1, rows, heads), 'ka', split_axis=2, concat_a...  8.19 us
    all_to_all x1, starting transfers between devices, local(): lax.all_to_all(total.reshape(1, rows, heads), 'ka', split_axis=2, concat_...  6.92 us
  transfers between devices with their start and end apart: 3, of which 2 were waited for; matrix products, arithmetic and copies ran while one was open for 12% of the time, Pallas kernels for 0%

profile of v1, /device:TPU:1, one launch (start us, length us, event | category | flops | bytes accessed | tf_op | source)
XLA Modules:
  0.0 171.7 jit_solution(12388889273287303156)
XLA Ops:
  0.7 1.5 reshape.516
  2.2 26.4 %all_gather.6 = bf16[1,2048,128]{2,1,0:T(8,128)(2,1)S(1)} all-gather(bf16[1,64,128]{2,1,0:T(8,128)(2,1)} %param.5), channel_id=1, replica_groups=mesh['pb'=32,'ka'=8] {'pb'}, dimensions={1}, use_global_device_ids=true | all-gather | bytes 540672 | tf_op jit(solution)/shard_map/all_gather | solution.py:57
  28.6 4.5 %fusion.46 = f32[4096,512]{0,1:T(8,128)} fusion(bf16[4096,128]{1,0:T(8,128)(2,1)S(1)} %reshape.516, bf16[1,2048,128]{2,1,0:T(8,128)(2,1)S(1)} %all_gather.6), kind=kOutput, calls=%fused_computation.69 | convolution fusion | flops 536870912 | bytes 9568256 | tf_op jit(solution)/shard_map/dot_general | solution.py:18
  33.1 4.5 %fusion.47 = f32[4096,512]{0,1:T(8,128)} fusion(bf16[4096,128]{1,0:T(8,128)(2,1)S(1)} %reshape.516, bf16[1,2048,128]{2,1,0:T(8,128)(2,1)S(1)} %all_gather.6), kind=kOutput, calls=%fused_computation.71 | convolution fusion | flops 536870912 | bytes 9568256 | tf_op jit(solution)/shard_map/dot_general | solution.py:18
  37.6 0.2 fusion.83
  37.9 0.1 broadcast_in_dim.101
  38.0 0.2 le.21
  38.1 0.2 select_reduce_fusion
  38.3 4.5 %fusion = (f32[4096]{0:T(1024)S(1)}, f32[4096,512]{0,1:T(8,128)}) fusion(s32[4096]{0:T(1024)S(1)} %le.21, s32[512]{0:T(512)S(1)} %get-tuple-element.31, bf16[4096,128]{1,0:T(8,128)(2,1)S(1)} %reshape.516, bf16[1,2048,128]{2,1,0:T(8,128)(2,1)S(1)} %all_gather.6), kind=kOutput, calls=%fused_computation.8 | convolution fusion | flops 545255424 | bytes 9603072 | tf_op jit(solution)/shard_map/dot_general | solution.py:18
  42.9 0.2 max_broadcast_in_dim.46
  43.0 15.8 %fusion.5 = (f32[4096]{0:T(1024)S(1)}, f32[4096]{0:T(1024)S(1)}, f32[4096]{0:T(1024)S(1)}, f32[4096]{0:T(1024)S(1)}, f32[4096,512]{0,1:T(8,128)}) fusion(f32[4096,512]{0,1:T(8,128)} %get-tuple-element.26, f32[4096]{0:T(1024)S(1)} %broadcast_maximum_fusion, s32[4096]{0:T(1024)S(1)} %le.21, s32[512]{0:T(512)S(1)} %get-tuple-element.31, ...), kind=kOutput, calls=%fused_computation.13 | convolution fusion | flops 572506112 | bytes 34840576 | tf_op jit(solution)/shard_map/dot_general | solution.py:18
  58.9 0.2 reduce_max.53
  59.0 0.2 reduce_max.55
  59.2 0.2 reduce_max.57
  59.4 0.1 copy.14
  59.5 0.1 copy.17
  59.6 0.1 copy.11
  59.7 11.3 %fusion.7 = (f32[4096]{0:T(1024)S(1)}, f32[4096]{0:T(1024)S(1)}, f32[4096]{0:T(1024)S(1)}) fusion(f32[4096,512]{0,1:T(8,128)} %get-tuple-element.27, f32[4096]{0:T(1024)S(1)} %get-tuple-element.23, s32[4096]{0:T(1024)S(1)} %le.21, s32[512]{0:T(512)S(1)} %get-tuple-element.28, f32[4096]{0:T(1024)S(1)} %get-tuple-element.21, f32[4096,512]{0,1:T(8,128)} %fusion.46, ...), kind=kLoop, calls=%fused_computation.15 | loop fusion | flops 31444992 | bytes 25286656 | tf_op jit(solution)/shard_map/reduce_sum | solution.py:27
  71.0 0.2 reduce_sum.113
  71.2 0.2 reduce_sum.116
  71.5 0.2 reduce_sum.119
  71.8 0.2 reduce_sum.110
  72.0 0.1 copy.19
  72.2 0.6 copy.22
  72.8 8.2 %all-to-all-start.1 = ((f32[1,512,8]{1,0,2:T(1,128)}), f32[1,512,8]{1,0,2:T(1,128)S(1)}, u32[]{:S(2)}, u32[]{:S(2)}) async-start(f32[1,512,8]{1,0,2:T(1,128)} %copy.22), calls=%async_computation.1 | async-start | bytes 32768 | tf_op jit(solution)/shard_map/all_to_all | solution.py:95
  81.1 24.7 %all_gather.7 = bf16[1,2048,128]{2,1,0:T(8,128)(2,1)S(1)} all-gather(bf16[1,64,128]{2,1,0:T(8,128)(2,1)S(1)} %copy-done), channel_id=1, replica_groups=mesh['pb'=32,'ka'=8] {'pb'}, dimensions={1}, use_global_device_ids=true | all-gather | bytes 540672 | tf_op jit(solution)/shard_map/all_gather | solution.py:58
  105.7 5.6 %fusion.14 = f32[4096,128]{1,0:T(8,128)S(1)} fusion(f32[4096,512]{0,1:T(8,128)} %get-tuple-element.26, f32[4096]{0:T(1024)S(1)} %broadcast_maximum_fusion, s32[4096]{0:T(1024)S(1)} %le.21, s32[512]{0:T(512)S(1)} %get-tuple-element.31, f32[4096]{0:T(1024)S(1)} %get-tuple-element.20, f32[4096]{0:T(1024)S(1)} %get-tuple-element.24, ...), kind=kOutput, calls=%fused_computation.26 | convolution fusion | flops 548405248 | bytes 10684416 | tf_op jit(solution)/shard_map/dot_general | solution.py:28
  111.4 2.6 %fusion.13 = f32[4096,128]{1,0:T(8,128)S(1)} fusion(f32[4096,128]{1,0:T(8,128)S(1)} %fusion.14, f32[4096,512]{0,1:T(8,128)S(1)} %bitcast.104, f32[4096]{0:T(1024)S(1)} %get-tuple-element.23, s32[4096]{0:T(1024)S(1)} %le.21, s32[512]{0:T(512)S(1)} %get-tuple-element.28, f32[4096]{0:T(1024)S(1)} %get-tuple-element.19, bf16[1,2048,128]{2,1,0:T(8,128)(2,1)S(1)} %all_gather.7), kind=kOutput, calls=%fused_computation.24 | convolution fusion | flops 548405248 | bytes 12765184 | tf_op jit(solution)/shard_map/dot_general | solution.py:28
  114.1 0.8 slice-done.3
  114.9 2.6 %fusion.12 = f32[4096,128]{1,0:T(8,128)S(1)} fusion(f32[4096,128]{1,0:T(8,128)S(1)} %fusion.13, f32[4096,512]{0,1:T(8,128)S(1)} %bitcast.102, f32[4096]{0:T(1024)S(1)} %get-tuple-element.22, s32[4096]{0:T(1024)S(1)} %le.21, s32[512]{0:T(512)S(1)} %get-tuple-element.29, f32[4096]{0:T(1024)S(1)} %get-tuple-element.18, bf16[1,2048,128]{2,1,0:T(8,128)(2,1)S(1)} %all_gather.7), kind=kOutput, calls=%fused_computation.22 | convolution fusion | flops 548405248 | bytes 12765184 | tf_op jit(solution)/shard_map/dot_general | solution.py:28
  117.6 2.6 %fusion.16 = bf16[4096,128]{1,0:T(8,128)(2,1)S(1)} fusion(f32[4096,128]{1,0:T(8,128)S(1)} %fusion.12, f32[4096,512]{0,1:T(8,128)S(1)} %bitcast.100, f32[4096]{0:T(1024)S(1)} %get-tuple-element.21, s32[4096]{0:T(1024)S(1)} %le.21, s32[512]{0:T(512)S(1)} %get-tuple-element.30, f32[4096]{0:T(1024)S(1)} %get-tuple-element.17, ...), kind=kOutput, calls=%fused_computation.28 | convolution fusion | flops 548929536 | bytes 11716608 | tf_op jit(solution)/shard_map/dot_general | solution.py:28
  120.2 0.5 reshape_reshape.2
  120.7 0.7 fusion.45
  121.4 0.7 fusion.44
  122.1 0.7 fusion.43
  122.8 0.7 fusion.42
  123.5 0.7 fusion.41
  124.2 0.7 fusion.40
  124.8 0.7 fusion.39
  125.5 0.6 copy.21
  126.2 6.9 %all-to-all-start = ((f32[1,512,8]{1,0,2:T(1,128)}), f32[1,512,8]{1,0,2:T(1,128)S(1)}, u32[]{:S(2)}, u32[]{:S(2)}) async-start(f32[1,512,8]{1,0,2:T(1,128)} %copy.21), calls=%async_computation | async-start | bytes 32768 | tf_op jit(solution)/shard_map/all_to_all | solution.py:96
  133.1 0.7 fusion.38
  133.8 5.9 %all-to-all-done = f32[1,512,8]{1,0,2:T(1,128)S(1)} async-done(((f32[1,512,8]{1,0,2:T(1,128)}), f32[1,512,8]{1,0,2:T(1,128)S(1)}, u32[]{:S(2)}, u32[]{:S(2)}) %all-to-all-start) | async-done | bytes 16416 | tf_op jit(solution)/shard_map/all_to_all | solution.py:96
  139.7 3.6 %all-to-all-start.2 = ((bf16[8,1,512,128]{3,2,1,0:T(8,128)(2,1)}), bf16[8,1,512,128]{3,2,1,0:T(8,128)(2,1)S(1)}, u32[]{:S(2)}, u32[]{:S(2)}) async-start(bf16[8,1,512,128]{3,2,1,0:T(8,128)(2,1)} %fusion.38), calls=%async_computation.2 | async-start | bytes 2097152 | tf_op jit(solution)/shard_map/all_to_all | solution.py:84
  143.3 0.6 log_add_fusion
  143.9 26.3 %all-to-all-done.2 = bf16[8,1,512,128]{3,2,1,0:T(8,128)(2,1)S(1)} async-done(((bf16[8,1,512,128]{3,2,1,0:T(8,128)(2,1)}), bf16[8,1,512,128]{3,2,1,0:T(8,128)(2,1)S(1)}, u32[]{:S(2)}, u32[]{:S(2)}) %all-to-all-start.2) | async-done | bytes 1048608 | tf_op jit(solution)/shard_map/all_to_all | solution.py:84
  170.2 0.7 fusion.37
  170.9 0.8 divide_convert_fusion
  (41 shorter events, 0.8 us)
Async XLA Ops:
  33.1 4.5 %copy-start.1 = (s32[64]{0:T(128)S(1)}, s32[64]{0:T(128)}, u32[]{:S(2)}) copy-start(s32[64]{0:T(128)} %param.7) | copy-start | bytes 772
  59.7 21.4 %copy-start = (bf16[1,64,128]{2,1,0:T(8,128)(2,1)S(1)}, bf16[1,64,128]{2,1,0:T(8,128)(2,1)}, u32[]{:S(2)}) copy-start(bf16[1,64,128]{2,1,0:T(8,128)(2,1)} %param.6) | copy-start | bytes 49156
  72.8 53.3 %all-to-all-start.1 = ((f32[1,512,8]{1,0,2:T(1,128)}), f32[1,512,8]{1,0,2:T(1,128)S(1)}, u32[]{:S(2)}, u32[]{:S(2)}) async-start(f32[1,512,8]{1,0,2:T(1,128)} %copy.22), calls=%async_computation.1 | async-start | bytes 32768 | tf_op jit(solution)/shard_map/all_to_all | solution.py:95
  81.0 30.4 %slice-start.4 = ((s8[8388608]{0:T(1024)(128)(4,1)}), s8[4194304]{0:T(1024)(128)(4,1)S(1)}, s32[]{:S(2)}) async-start(s8[8388608]{0:T(1024)(128)(4,1)} %bitcast.103), calls=%async_computation.7 | async-start | bytes 8388608
  105.7 5.7 %slice-start.5 = ((s8[8388608]{0:T(1024)(128)(4,1)}), s8[4194304]{0:T(1024)(128)(4,1)S(1)}, s32[]{:S(2)}) async-start(s8[8388608]{0:T(1024)(128)(4,1)} %bitcast.103), calls=%async_computation.8 | async-start | bytes 8388608
  111.4 2.7 %slice-start.2 = ((s8[8388608]{0:T(1024)(128)(4,1)}), s8[4194304]{0:T(1024)(128)(4,1)S(1)}, s32[]{:S(2)}) async-start(s8[8388608]{0:T(1024)(128)(4,1)} %bitcast.101), calls=%async_computation.5 | async-start | bytes 8388608
  111.4 3.4 %slice-start.3 = ((s8[8388608]{0:T(1024)(128)(4,1)}), s8[4194304]{0:T(1024)(128)(4,1)S(1)}, s32[]{:S(2)}) async-start(s8[8388608]{0:T(1024)(128)(4,1)} %bitcast.101), calls=%async_computation.6 | async-start | bytes 8388608
  114.1 3.4 %slice-start = ((s8[8388608]{0:T(1024)(128)(4,1)}), s8[4194304]{0:T(1024)(128)(4,1)S(1)}, s32[]{:S(2)}) async-start(s8[8388608]{0:T(1024)(128)(4,1)} %bitcast.99), calls=%async_computation.3 | async-start | bytes 8388608
  114.9 2.7 %slice-start.1 = ((s8[8388608]{0:T(1024)(128)(4,1)}), s8[4194304]{0:T(1024)(128)(4,1)S(1)}, s32[]{:S(2)}) async-start(s8[8388608]{0:T(1024)(128)(4,1)} %bitcast.99), calls=%async_computation.4 | async-start | bytes 8388608
  126.2 13.5 %all-to-all-start = ((f32[1,512,8]{1,0,2:T(1,128)}), f32[1,512,8]{1,0,2:T(1,128)S(1)}, u32[]{:S(2)}, u32[]{:S(2)}) async-start(f32[1,512,8]{1,0,2:T(1,128)} %copy.21), calls=%async_computation | async-start | bytes 32768 | tf_op jit(solution)/shard_map/all_to_all | solution.py:96
  139.7 30.5 %all-to-all-start.2 = ((bf16[8,1,512,128]{3,2,1,0:T(8,128)(2,1)}), bf16[8,1,512,128]{3,2,1,0:T(8,128)(2,1)S(1)}, u32[]{:S(2)}, u32[]{:S(2)}) async-start(bf16[8,1,512,128]{3,2,1,0:T(8,128)(2,1)} %fusion.38), calls=%async_computation.2 | async-start | bytes 2097152 | tf_op jit(solution)/shard_map/all_to_all | solution.py:84
